TPU v7x, 32 devices: a whole 2x2x4 slice. The times are simulated.
32 devices in a mesh: pipe: 4 (over z), blk: 2 (over x), uly: 4 (over y, core).
Axes of the slice: x: 2, y: 2, z: 4, core: 2. Of those that a mesh axis runs over, the one named last changes fastest.
Arguments:
- hidden_in: bfloat16 [4, 64, 3072], P('pipe', ('blk', 'uly')), may hold values from -6 to 6
- text_len: int32 [1], replicated, may hold values from 16 to 64
- qkv_video: bfloat16 [4, 3072, 3, 1536], P('pipe', 'blk', None, 'uly'), may hold values from -0.109375 to 0.109375
- qkv_text: bfloat16 [2, 3072, 3, 1536], P(None, 'blk', None, 'uly'), may hold values from -0.109375 to 0.109375
- out_video: bfloat16 [4, 1536, 3072], P('pipe', 'uly', 'blk'), may hold values from -0.15625 to 0.15625
- out_text: bfloat16 [2, 1536, 3072], P(None, 'uly', 'blk'), may hold values from -0.15625 to 0.15625
- modulation: float32 [4, 2, 3, 3072], P('pipe'), may hold values from -3 to 3
- qk_gain: float32 [4, 2, 2, 128], P('pipe'), may hold values from 1 to 3
- stale_kv: bfloat16 [4, 2, 256, 1536], P('pipe', None, None, 'uly'), may hold values from -24 to 24, as said below
Outputs:
- hidden_out: bfloat16 [4, 64, 3072], P('pipe', ('blk', 'uly'))
Inputs may be any that keep to these rules, and one draw needn't show every extreme that they name: `stale_kv`: stale keys and values of order one, some keys larger.
All inputs are finite; a program needn't handle non-finite values.
Results may differ from a plain program's by a relative error of at most 0.04.
Values may be sent and summed in bfloat16 or wider, within the bound.
A program may use at most 128 MiB of HBM per device.

v0:
```python
import math
import jax
import jax.numpy as jnp
from jax import lax
from jax.sharding import PartitionSpec as P


def from_behind(shard, axis, by):
    size = lax.axis_size(axis)
    pairs = [(i, i + by) for i in range(size) if 0 <= i + by < size]
    return lax.ppermute(shard, axis, pairs)


def rms_scale(values, gain):
    squares = jnp.mean(values * values, axis=-1, keepdims=True)
    return values * lax.rsqrt(squares + 1e-06) * gain


def local(
    hidden_in, text_len, qkv_video, qkv_text, out_video, out_text, modulation, qk_gain, stale_kv
):
    sections = lax.axis_size("pipe")
    blk_count = lax.axis_size("blk")
    uly_count = lax.axis_size("uly")
    section = lax.axis_index("pipe")
    blk_index = lax.axis_index("blk")
    rows = hidden_in.shape[1]
    width = hidden_in.shape[2]
    group = rows * uly_count
    micro = group * blk_count
    text_count = 2 * group
    dual_count = qkv_text.shape[0]
    head_dim = qk_gain.shape[3]
    local_width = stale_kv.shape[3]
    local_heads = local_width // head_dim
    inv_scale = 1.0 / math.sqrt(head_dim)
    dual = section < dual_count
    chosen = jnp.minimum(section, dual_count - 1)
    text_rows_w = lax.dynamic_index_in_dim(qkv_text, chosen, 0, keepdims=False)
    text_cols_w = lax.dynamic_index_in_dim(out_text, chosen, 0, keepdims=False)
    video_proj, text_proj, video_back, text_back = (
        lax.all_gather(qkv_video[0], "blk", axis=0, tiled=True),
        lax.all_gather(text_rows_w, "blk", axis=0, tiled=True),
        lax.all_gather(out_video[0], "blk", axis=1, tiled=True),
        lax.all_gather(text_cols_w, "blk", axis=1, tiled=True),
    )
    video_proj = video_proj.reshape(width, 3 * local_width)
    text_proj = text_proj.reshape(width, 3 * local_width)
    mods = modulation[0]
    gains = qk_gain[0]
    stale = stale_kv[0]
    valid_text = text_len[0]
    cache_keys = stale[0]
    cache_values = stale[1]
    places = jnp.arange(micro * sections, dtype=jnp.int32)
    key_ok = (places >= text_count) | (places < valid_text)
    carried = jnp.zeros((rows, width), jnp.bfloat16)
    inbox = hidden_in[0]
    outbox = jnp.zeros((rows, width), jnp.bfloat16)
    last_tick = 2 * sections - 2
    for tick in range(2 * sections - 1):
        micro_index = tick - section
        valid = (micro_index >= 0) & (micro_index < sections)
        current = jnp.clip(micro_index, 0, sections - 1)
        entering = jnp.where(section == 0, inbox, carried)
        is_text = dual & (current * micro + blk_index * group < text_count)
        stream = is_text.astype(jnp.int32)
        mod_rows = lax.dynamic_index_in_dim(mods, stream, 0, keepdims=False)
        gain_rows = lax.dynamic_index_in_dim(gains, stream, 0, keepdims=False)
        floats = entering.astype(jnp.float32)
        centred = floats - jnp.mean(floats, axis=-1, keepdims=True)
        normed = centred * lax.rsqrt(jnp.mean(centred * centred, axis=-1, keepdims=True) + 1e-06)
        modded = (normed * (1.0 + mod_rows[1]) + mod_rows[0]).astype(jnp.bfloat16)
        gathered = lax.all_gather(modded, "uly", axis=0, tiled=True)
        projected = lax.cond(
            is_text,
            lambda operand: jnp.dot(operand, text_proj, preferred_element_type=jnp.float32),
            lambda operand: jnp.dot(operand, video_proj, preferred_element_type=jnp.float32),
            gathered,
        )
        projected = projected.reshape(group, 3, local_heads, head_dim)
        queries = rms_scale(projected[:, 0], gain_rows[0]).astype(jnp.bfloat16)
        fresh_keys = (
            rms_scale(projected[:, 1], gain_rows[1])
            .astype(jnp.bfloat16)
            .reshape(group, local_width)
        )
        fresh_values = projected[:, 2].astype(jnp.bfloat16).reshape(group, local_width)
        all_keys, all_values = (
            lax.all_gather(fresh_keys, "blk", axis=0, tiled=True),
            lax.all_gather(fresh_values, "blk", axis=0, tiled=True),
        )
        offset = current * micro
        old_keys = lax.dynamic_slice_in_dim(cache_keys, offset, micro, 0)
        old_values = lax.dynamic_slice_in_dim(cache_values, offset, micro, 0)
        cache_keys = lax.dynamic_update_slice_in_dim(
            cache_keys, jnp.where(valid, all_keys, old_keys), offset, 0
        )
        cache_values = lax.dynamic_update_slice_in_dim(
            cache_values, jnp.where(valid, all_values, old_values), offset, 0
        )
        key_heads = cache_keys.reshape(-1, local_heads, head_dim)
        value_heads = cache_values.reshape(-1, local_heads, head_dim)
        scores = (
            jnp.einsum("rhd,lhd->hrl", queries, key_heads, preferred_element_type=jnp.float32)
            * inv_scale
        )
        scores = jnp.where(key_ok[None, None, :], scores, -1e30)
        peak = jnp.max(scores, axis=-1, keepdims=True)
        weights = jnp.where(key_ok[None, None, :], jnp.exp(scores - peak), 0.0)
        total = jnp.sum(weights, axis=-1)
        mixed = jnp.einsum(
            "hrl,lhd->rhd",
            weights.astype(jnp.bfloat16),
            value_heads,
            preferred_element_type=jnp.float32,
        )
        attended = (
            (mixed / jnp.transpose(total)[:, :, None])
            .reshape(group, local_width)
            .astype(jnp.bfloat16)
        )
        partial_value = lax.cond(
            is_text,
            lambda operand: jnp.dot(operand, text_back, preferred_element_type=jnp.float32),
            lambda operand: jnp.dot(operand, video_back, preferred_element_type=jnp.float32),
            attended,
        )
        summed = lax.psum_scatter(partial_value, "uly", scatter_dimension=0, tiled=True)
        leaving = (floats + mod_rows[2] * summed).astype(jnp.bfloat16)
        outbox = jnp.where((section == sections - 1) & valid, leaving, outbox)
        if tick < last_tick:
            carried = from_behind(leaving, "pipe", 1)
            inbox, outbox = from_behind((inbox, outbox), "pipe", -1)
    return outbox[None]


def solution(mesh):
    return jax.shard_map(
        local,
        mesh=mesh,
        in_specs=(
            P("pipe", ("blk", "uly"), None),
            P(),
            P("pipe", "blk", None, "uly"),
            P(None, "blk", None, "uly"),
            P("pipe", "uly", "blk"),
            P(None, "uly", "blk"),
            P("pipe", None, None, None),
            P("pipe", None, None, None),
            P("pipe", None, None, "uly"),
        ),
        out_specs=P("pipe", ("blk", "uly"), None),
        check_vma=False,
    )
```

profile of v0, /device:TPU:0, one launch (start us, length us, event | category | flops | bytes accessed | tf_op | source)
XLA Modules:
  0.0 631.8 jit_solution(11148494798743195502)
XLA Ops:
  6.5 4.2 constant_dynamic-slice_fusion.23
  10.8 6.1 copy.199
  16.9 6.1 copy.109
  30.0 6.9 %all_gather.75 = bf16[32,3072]{1,0:T(8,128)(2,1)S(1)} all-gather(bf16[8,3072]{1,0:T(8,128)(2,1)S(1)} %fusion.97), channel_id=1, replica_groups=mesh['pipe'=4,'blk'=2,'uly'=4] {'uly'}, dimensions={0}, use_global_device_ids=true | all-gather | bytes 245760 | tf_op jit(solution)/shard_map/all_gather | solution.py:74
  36.9 72.1 %all-gather.11.cloned.1.call-done = bf16[1,3072,3,384]{1,3,2,0:T(8,128)(2,1)} async-done(((bf16[1,1536,3,384]{1,3,2,0:T(8,128)(2,1)}), bf16[1,3072,3,384]{1,3,2,0:T(8,128)(2,1)}) %all-gather.11.cloned.1.call-update) | async-done | bytes 7077904 | tf_op jit(solution)/shard_map/all_gather | solution.py:43
  109.0 90.8 %all-gather.9.cloned.1.call-done = bf16[1,3072,3,384]{1,3,2,0:T(8,128)(2,1)} async-done(((bf16[1,1536,3,384]{1,3,2,0:T(8,128)(2,1)}), bf16[1,3072,3,384]{1,3,2,0:T(8,128)(2,1)}) %all-gather.9.cloned.1.call-update) | async-done | bytes 7077904 | tf_op jit(solution)/shard_map/all_gather | solution.py:42
  199.8 5.2 conditional.14
  199.8 5.2 fusion.171
  205.3 4.5 all_gather.79
  209.9 5.0 all_gather.78
  216.8 21.1 %all-gather.15.cloned.1.call-done = bf16[1,384,3072]{2,1,0:T(8,128)(2,1)} async-done(((bf16[1,384,1536]{2,1,0:T(8,128)(2,1)}), bf16[1,384,3072]{2,1,0:T(8,128)(2,1)}) %all-gather.15.cloned.1.call-update) | async-done | bytes 2359312 | tf_op jit(solution)/shard_map/all_gather | solution.py:45
  237.9 37.5 %all-gather.13.cloned.1.call-done = bf16[1,384,3072]{2,1,0:T(8,128)(2,1)} async-done(((bf16[1,384,1536]{2,1,0:T(8,128)(2,1)}), bf16[1,384,3072]{2,1,0:T(8,128)(2,1)}) %all-gather.13.cloned.1.call-update) | async-done | bytes 2359312 | tf_op jit(solution)/shard_map/all_gather | solution.py:44
  279.7 19.6 %reduce-scatter.8.cloned.1.call-done = f32[8,3072]{1,0:T(8,128)} async-done(((f32[32,3072]{1,0:T(8,128)}), f32[8,3072]{1,0:T(8,128)}) %reduce-scatter.8.cloned.1.call-update) | async-done | bytes 98320 | tf_op jit(solution)/shard_map/reduce_scatter | solution.py:129
  300.2 3.4 collective-permute-start.6
  305.8 5.6 all_gather.82
  311.4 5.2 conditional.16
  311.4 5.2 fusion.174
  317.1 5.0 all_gather.84
  323.1 4.5 all_gather.83
  335.4 2.9 collective-permute-done.12
  338.3 15.1 %reduce-scatter.10.cloned.1.call-done = f32[8,3072]{1,0:T(8,128)} async-done(((f32[32,3072]{1,0:T(8,128)}), f32[8,3072]{1,0:T(8,128)}) %reduce-scatter.10.cloned.1.call-update) | async-done | bytes 98320 | tf_op jit(solution)/shard_map/reduce_scatter | solution.py:129
  354.3 3.4 collective-permute-start.7
  360.6 5.6 all_gather.85
  366.2 5.2 conditional.18
  366.2 5.2 fusion.178
  371.9 4.5 all_gather.87
  377.0 4.5 all_gather.86
  382.8 2.2 conditional.19
  388.9 4.4 collective-permute-done.13
  393.2 14.4 %reduce-scatter.12.cloned.1.call-done = f32[8,3072]{1,0:T(8,128)} async-done(((f32[32,3072]{1,0:T(8,128)}), f32[8,3072]{1,0:T(8,128)}) %reduce-scatter.12.cloned.1.call-update) | async-done | bytes 98320 | tf_op jit(solution)/shard_map/reduce_scatter | solution.py:129
  408.6 3.4 collective-permute-start.8
  414.2 5.6 all_gather.88
  419.8 5.2 conditional.20
  419.8 5.2 fusion.182
  425.5 4.7 all_gather.90
  431.1 4.5 all_gather.89
  442.9 3.4 collective-permute-done.14
  446.2 15.2 %reduce-scatter.14.cloned.1.call-done = f32[8,3072]{1,0:T(8,128)} async-done(((f32[32,3072]{1,0:T(8,128)}), f32[8,3072]{1,0:T(8,128)}) %reduce-scatter.14.cloned.1.call-update) | async-done | bytes 98320 | tf_op jit(solution)/shard_map/reduce_scatter | solution.py:129
  462.4 3.4 collective-permute-start.9
  468.0 5.6 all_gather.91
  473.6 5.2 conditional.22
  473.6 5.2 fusion.186
  479.2 4.5 all_gather.93
  484.7 4.5 all_gather.92
  490.8 2.2 conditional.23
  496.4 3.7 collective-permute-done.15
  500.1 15.6 %reduce-scatter.16.cloned.1.call-done = f32[8,3072]{1,0:T(8,128)} async-done(((f32[32,3072]{1,0:T(8,128)}), f32[8,3072]{1,0:T(8,128)}) %reduce-scatter.16.cloned.1.call-update) | async-done | bytes 98320 | tf_op jit(solution)/shard_map/reduce_scatter | solution.py:129
  516.6 3.4 collective-permute-start.10
  522.2 5.6 all_gather.94
  527.8 5.2 conditional.24
  527.8 5.2 fusion.190
  533.5 4.7 all_gather.96
  539.1 4.5 all_gather.95
  550.9 3.7 collective-permute-done.16
  554.6 14.8 %reduce-scatter.18.cloned.1.call-done = f32[8,3072]{1,0:T(8,128)} async-done(((f32[32,3072]{1,0:T(8,128)}), f32[8,3072]{1,0:T(8,128)}) %reduce-scatter.18.cloned.1.call-update) | async-done | bytes 98320 | tf_op jit(solution)/shard_map/reduce_scatter | solution.py:129
  570.3 3.4 collective-permute-start.11
  575.9 5.6 all_gather.97
  581.5 5.2 conditional.26
  581.5 5.2 fusion.194
  587.1 4.5 all_gather.99
  592.6 4.5 all_gather.98
  598.7 2.2 conditional.27
  603.0 5.0 collective-permute-done.17
  608.0 15.5 %reduce-scatter.20.cloned.1.call-done = f32[8,3072]{1,0:T(8,128)} async-done(((f32[32,3072]{1,0:T(8,128)}), f32[8,3072]{1,0:T(8,128)}) %reduce-scatter.20.cloned.1.call-update) | async-done | bytes 98320 | tf_op jit(solution)/shard_map/reduce_scatter | solution.py:129
  (302 shorter events, 92.1 us)
Async XLA Ops:
  6.5 16.6 %copy-start = (bf16[2,384,1536]{2,1,0:T(8,128)(2,1)S(1)}, bf16[2,384,1536]{2,1,0:T(8,128)(2,1)}, u32[]{:S(2)}) copy-start(bf16[2,384,1536]{2,1,0:T(8,128)(2,1)} %param.42) | copy-start | bytes 7077892
  6.5 102.5 %all-gather.11.cloned.1.call-start = ((), (), s32[]{:S(2)}) async-start(), calls=%async_computation.15 | async-start | bytes 10616832 | tf_op jit(solution)/shard_map/all_gather | solution.py:43
  16.9 182.9 %all-gather.9.cloned.1.call-start = ((), (), s32[]{:S(2)}) async-start(), calls=%async_computation.14 | async-start | bytes 10616832 | tf_op jit(solution)/shard_map/all_gather | solution.py:42
  23.0 1.9 copy-start.9
  23.1 5.4 copy-start.11
  23.1 6.0 copy-start.8
  23.1 214.8 %all-gather.15.cloned.1.call-start = ((), (), s32[]{:S(2)}) async-start(), calls=%async_computation.17 | async-start | bytes 3538944 | tf_op jit(solution)/shard_map/all_gather | solution.py:45
  24.3 251.1 %all-gather.13.cloned.1.call-start = ((), (), s32[]{:S(2)}) async-start(), calls=%async_computation.16 | async-start | bytes 3538944 | tf_op jit(solution)/shard_map/all_gather | solution.py:44
  24.9 274.4 %reduce-scatter.8.cloned.1.call-start = ((), (), s32[]{:S(2)}) async-start(), calls=%async_computation.7 | async-start | bytes 491520 | tf_op jit(solution)/shard_map/reduce_scatter | solution.py:129
  199.8 16.4 %copy-start.19 = (pred[256]{0:T(512)(128)(4,1)S(1)}, pred[256]{0:T(512)(128)(4,1)}, u32[]{:S(2)}) copy-start(pred[256]{0:T(512)(128)(4,1)} %compare_or_fusion) | copy-start | bytes 772
  216.0 63.7 %copy-start.16 = (f32[1,1,2,128]{3,2,1,0:T(2,128)S(1)}, f32[1,1,2,128]{3,2,1,0:T(2,128)}, u32[]{:S(2)}) copy-start(f32[1,1,2,128]{3,2,1,0:T(2,128)} %get-tuple-element.336) | copy-start | bytes 3076
  277.5 0.8 copy-start.1
  278.3 75.1 %reduce-scatter.10.cloned.1.call-start = ((), (), s32[]{:S(2)}) async-start(), calls=%async_computation.8 | async-start | bytes 491520 | tf_op jit(solution)/shard_map/reduce_scatter | solution.py:129
  278.4 25.3 %collective-permute-start = (bf16[8,3072]{1,0:T(8,128)(2,1)S(1)}, bf16[8,3072]{1,0:T(8,128)(2,1)S(1)}, u32[]{:S(2)}, u32[]{:S(2)}) collective-permute-start(bf16[8,3072]{1,0:T(8,128)(2,1)S(1)} %bitcast.470), channel_id=1, source_target_pairs={{8,0},{16,8},{24,16},{9,1},{17,9},{25,17},{10,2},{18,10},{26,18},{... | collective-permute-start | bytes 147464 | tf_op jit(solution)/shard_map/ppermute | solution.py:11
  300.2 5.1 collective-permute-start.6
  311.4 17.3 %copy-start.20 = (pred[256]{0:T(512)(128)(4,1)S(1)}, pred[256]{0:T(512)(128)(4,1)}, u32[]{:S(2)}) copy-start(pred[256]{0:T(512)(128)(4,1)} %compare_or_fusion) | copy-start | bytes 772
  327.8 5.8 copy-start.15
  331.4 0.7 copy-start.2
  332.2 75.5 %reduce-scatter.12.cloned.1.call-start = ((), (), s32[]{:S(2)}) async-start(), calls=%async_computation.9 | async-start | bytes 491520 | tf_op jit(solution)/shard_map/reduce_scatter | solution.py:129
  332.3 6.0 collective-permute-start.12
  334.1 23.6 %collective-permute-start.1 = (bf16[8,3072]{1,0:T(8,128)(2,1)S(1)}, bf16[8,3072]{1,0:T(8,128)(2,1)S(1)}, u32[]{:S(2)}, u32[]{:S(2)}) collective-permute-start(bf16[8,3072]{1,0:T(8,128)(2,1)S(1)} %collective-permute-done), channel_id=1, source_target_pairs={{8,0},{16,8},{24,16},{9,1},{17,9},{25,17},{10,2},{18,10},{26,18},{... | collective-permute-start | bytes 147464 | tf_op jit(solution)/shard_map/ppermute | solution.py:11
  354.3 5.1 collective-permute-start.7
  366.2 15.9 %copy-start.17 = (f32[128]{0:T(128)S(1)}, f32[128]{0:T(128)}, u32[]{:S(2)}) copy-start(f32[128]{0:T(128)} %get-tuple-element.347) | copy-start | bytes 1540
  366.2 16.0 %copy-start.21 = (pred[256]{0:T(512)(128)(4,1)S(1)}, pred[256]{0:T(512)(128)(4,1)}, u32[]{:S(2)}) copy-start(pred[256]{0:T(512)(128)(4,1)} %compare_or_fusion) | copy-start | bytes 772
  381.7 5.4 copy-start.14
  382.5 31.5 %copy-start.10 = (f32[1,1,1,3072]{3,1,2,0:T(1,128)S(1)}, f32[1,1,1,3072]{3,1,2,0:T(1,128)}, u32[]{:S(2)}) copy-start(f32[1,1,1,3072]{3,1,2,0:T(1,128)} %get-tuple-element.326) | copy-start | bytes 36868
  385.0 0.7 copy-start.3
  385.7 75.7 %reduce-scatter.14.cloned.1.call-start = ((), (), s32[]{:S(2)}) async-start(), calls=%async_computation.10 | async-start | bytes 491520 | tf_op jit(solution)/shard_map/reduce_scatter | solution.py:129
  385.8 7.5 %collective-permute-start.13 = (bf16[8,3072]{1,0:T(8,128)(2,1)S(1)}, bf16[8,3072]{1,0:T(8,128)(2,1)S(1)}, u32[]{:S(2)}, u32[]{:S(2)}) collective-permute-start(bf16[8,3072]{1,0:T(8,128)(2,1)S(1)} %get-tuple-element.281), channel_id=1, source_target_pairs={{8,0},{16,8},{24,16},{9,1},{17,9},{25,17},{10,2},{18,10},{26,18},{... | collective-permute-start | bytes 147464 | tf_op jit(solution)/shard_map/ppermute | solution.py:11
  387.6 24.4 %collective-permute-start.2 = (bf16[8,3072]{1,0:T(8,128)(2,1)S(1)}, bf16[8,3072]{1,0:T(8,128)(2,1)S(1)}, u32[]{:S(2)}, u32[]{:S(2)}) collective-permute-start(bf16[8,3072]{1,0:T(8,128)(2,1)S(1)} %collective-permute-done.1), channel_id=1, source_target_pairs={{8,0},{16,8},{24,16},{9,1},{17,9},{25,17},{10,2},{18,10},{26,18},{... | collective-permute-start | bytes 147464 | tf_op jit(solution)/shard_map/ppermute | solution.py:11
  408.6 5.1 collective-permute-start.8
  419.8 16.8 %copy-start.18 = (f32[128]{0:T(128)S(1)}, f32[128]{0:T(128)}, u32[]{:S(2)}) copy-start(f32[128]{0:T(128)} %get-tuple-element.345) | copy-start | bytes 1540
  419.8 16.9 %copy-start.22 = (pred[256]{0:T(512)(128)(4,1)S(1)}, pred[256]{0:T(512)(128)(4,1)}, u32[]{:S(2)}) copy-start(pred[256]{0:T(512)(128)(4,1)} %compare_or_fusion) | copy-start | bytes 772
  435.8 5.7 copy-start.13
  439.4 0.7 copy-start.4
  440.2 75.5 %reduce-scatter.16.cloned.1.call-start = ((), (), s32[]{:S(2)}) async-start(), calls=%async_computation.11 | async-start | bytes 491520 | tf_op jit(solution)/shard_map/reduce_scatter | solution.py:129
  440.2 6.0 collective-permute-start.14
  441.6 24.3 %collective-permute-start.3 = (bf16[8,3072]{1,0:T(8,128)(2,1)S(1)}, bf16[8,3072]{1,0:T(8,128)(2,1)S(1)}, u32[]{:S(2)}, u32[]{:S(2)}) collective-permute-start(bf16[8,3072]{1,0:T(8,128)(2,1)S(1)} %collective-permute-done.2), channel_id=1, source_target_pairs={{8,0},{16,8},{24,16},{9,1},{17,9},{25,17},{10,2},{18,10},{26,18},{... | collective-permute-start | bytes 147464 | tf_op jit(solution)/shard_map/ppermute | solution.py:11
  462.4 5.1 collective-permute-start.9
  489.4 5.7 copy-start.12
  493.0 0.7 copy-start.5
  493.8 75.6 %reduce-scatter.18.cloned.1.call-start = ((), (), s32[]{:S(2)}) async-start(), calls=%async_computation.12 | async-start | bytes 491520 | tf_op jit(solution)/shard_map/reduce_scatter | solution.py:129
  493.8 6.3 collective-permute-start.15
  495.1 24.9 %collective-permute-start.4 = (bf16[8,3072]{1,0:T(8,128)(2,1)S(1)}, bf16[8,3072]{1,0:T(8,128)(2,1)S(1)}, u32[]{:S(2)}, u32[]{:S(2)}) collective-permute-start(bf16[8,3072]{1,0:T(8,128)(2,1)S(1)} %collective-permute-done.3), channel_id=1, source_target_pairs={{8,0},{16,8},{24,16},{9,1},{17,9},{25,17},{10,2},{18,10},{26,18},{... | collective-permute-start | bytes 147464 | tf_op jit(solution)/shard_map/ppermute | solution.py:11
  516.6 5.1 collective-permute-start.10
  547.4 0.7 copy-start.6
  548.2 75.3 %reduce-scatter.20.cloned.1.call-start = ((), (), s32[]{:S(2)}) async-start(), calls=%async_computation.13 | async-start | bytes 491520 | tf_op jit(solution)/shard_map/reduce_scatter | solution.py:129
  548.3 6.3 collective-permute-start.16
  549.6 24.1 %collective-permute-start.5 = (bf16[8,3072]{1,0:T(8,128)(2,1)S(1)}, bf16[8,3072]{1,0:T(8,128)(2,1)S(1)}, u32[]{:S(2)}, u32[]{:S(2)}) collective-permute-start(bf16[8,3072]{1,0:T(8,128)(2,1)S(1)} %collective-permute-done.4), channel_id=1, source_target_pairs={{8,0},{16,8},{24,16},{9,1},{17,9},{25,17},{10,2},{18,10},{26,18},{... | collective-permute-start | bytes 147464 | tf_op jit(solution)/shard_map/ppermute | solution.py:11
  570.3 5.1 collective-permute-start.11
  600.9 0.8 copy-start.7
  601.7 6.3 collective-permute-start.17
Sparse Core Ops, SparseCore 0:
  17.0 91.9 all-gather.10
  110.5 89.2 all-gather.8
  201.4 36.4 all-gather.14
  239.2 36.0 all-gather.12
  278.4 20.8 reduce-scatter.7
  332.3 20.9 reduce-scatter.9
  385.8 21.7 reduce-scatter.11
  440.3 21.1 reduce-scatter.13
  493.9 21.7 reduce-scatter.15
  548.3 20.9 reduce-scatter.17
  601.8 21.6 reduce-scatter.19
where the time goes:
time: 641 us; the launch traced here: 632 us
  waiting for transfers between devices  366 us (57%)
  blocking collectives  105 us (16%)
  matrix products  55.1 us (9%)
  local copies, waits for them, and re-layouts  38 us (6%)
  starting transfers between devices  36.3 us (6%)
  other arithmetic  16 us (2%)
  between operations  15.7 us (2%)
    reduce_scatter x7, waiting for transfers between devices, local(): lax.psum_scatter(partial_value, 'uly', scatter_dimension=0, tiled=True)  110 us
    all_gather x1, waiting for transfers between devices, local(): lax.all_gather(qkv_video[0], 'blk', axis=0, tiled=True)  90.8 us
    all_gather x1, waiting for transfers between devices, local(): lax.all_gather(text_rows_w, 'blk', axis=0, tiled=True)  72.1 us
    all_gather x7, blocking collectives, local(): gathered = lax.all_gather(modded, 'uly', axis=0, tiled=True)  40.5 us
    all_gather x1, waiting for transfers between devices, local(): lax.all_gather(out_video[0], 'blk', axis=1, tiled=True)  37.5 us
    ppermute x18, starting transfers between devices, from_behind(): return lax.ppermute(shard, axis, pairs)  35.8 us
    ppermute x18, waiting for transfers between devices, from_behind(): return lax.ppermute(shard, axis, pairs)  33.3 us
    all_gather x7, blocking collectives, local(): lax.all_gather(fresh_keys, 'blk', axis=0, tiled=True)  32.4 us
  transfers between devices with their start and end apart: 29, of which 23 were waited for; matrix products, arithmetic and copies ran while one was open for 4% of the time, Pallas kernels for 0%

commit v1 on v0

--- a/solution.py
+++ b/solution.py
@@ -3,6 +3,27 @@
 import jax.numpy as jnp
 from jax import lax
 from jax.sharding import PartitionSpec as P
+
+
+def joined_along(parts, dim):
+    shape = list(parts.shape[1:])
+    shape[dim] *= parts.shape[0]
+    return jnp.moveaxis(parts, 0, dim).reshape(shape)
+
+
+def doubled(array, axis):
+    length, index = (lax.axis_size(axis), lax.axis_index(axis))
+    blocks, apart = (array[None], 1)
+    while apart < length:
+        theirs = lax.ppermute(blocks, axis, [(i, i ^ apart) for i in range(length)])
+        low = index & apart == 0
+        blocks = jnp.concatenate([jnp.where(low, blocks, theirs), jnp.where(low, theirs, blocks)])
+        apart *= 2
+    return blocks
+
+
+def gather_by_bits(x, axis, dim):
+    return joined_along(doubled(x, axis), dim)
 
 
 def from_behind(shard, axis, by):
@@ -41,7 +62,7 @@
     video_proj, text_proj, video_back, text_back = (
         lax.all_gather(qkv_video[0], "blk", axis=0, tiled=True),
         lax.all_gather(text_rows_w, "blk", axis=0, tiled=True),
-        lax.all_gather(out_video[0], "blk", axis=1, tiled=True),
+        gather_by_bits(out_video[0], "blk", 1),
         lax.all_gather(text_cols_w, "blk", axis=1, tiled=True),
     )
     video_proj = video_proj.reshape(width, 3 * local_width)

time: 641 us -> 617 us (0.963)
  waiting for transfers between devices: 366 us -> 343 us
  matrix products: 55.1 us -> 47.7 us
    all_gather x1 -> x0, waiting for transfers between devices: 37.5 us -> none  [local(): lax.all_gather(out_video[0], 'blk', axis=1, tiled=True)]
    ppermute x0 -> x1, waiting for transfers between devices: none -> 36 us  [doubled(): theirs = lax.ppermute(blocks, axis, [(i, i ^ apart) for i in range(length)])]
    all_gather x1, waiting for transfers between devices: 72.1 us -> 52.6 us  [local(): lax.all_gather(text_rows_w, 'blk', axis=0, tiled=True)]
    dot_general x6, matrix products: 13.1 us -> 4.95 us  [local(): jnp.dot(operand, video_back, preferred_element_type=jnp.float32)]
    unnamed x57 -> x59, local copies, waits for them, and re-layouts: 17.8 us -> 17.9 us
  transfers between devices with their start and end apart: 29 -> 29, of which waited for: 23 -> 23; matrix products, arithmetic and copies ran while one was open for 4% -> 5% of each run, Pallas kernels for 0% -> 0%
where the time goes in v1:
time: 617 us; the launch traced here: 607 us
  waiting for transfers between devices  343 us (56%)
  blocking collectives  104 us (17%)
  matrix products  47.7 us (8%)
  starting transfers between devices  39.2 us (6%)
  local copies, waits for them, and re-layouts  38.4 us (6%)
  other arithmetic  18.7 us (3%)
  between operations  16 us (3%)
    reduce_scatter x7, waiting for transfers between devices, local(): lax.psum_scatter(partial_value, 'uly', scatter_dimension=0, tiled=True)  107 us
    all_gather x1, waiting for transfers between devices, local(): lax.all_gather(qkv_video[0], 'blk', axis=0, tiled=True)  92.3 us
    all_gather x1, waiting for transfers between devices, local(): lax.all_gather(text_rows_w, 'blk', axis=0, tiled=True)  52.6 us
    all_gather x7, blocking collectives, local(): gathered = lax.all_gather(modded, 'uly', axis=0, tiled=True)  39.2 us
    ppermute x1, waiting for transfers between devices, doubled(): theirs = lax.ppermute(blocks, axis, [(i, i ^ apart) for i in range(length)])  36 us
    ppermute x18, starting transfers between devices, from_behind(): return lax.ppermute(shard, axis, pairs)  35.8 us
    ppermute x18, waiting for transfers between devices, from_behind(): return lax.ppermute(shard, axis, pairs)  34.8 us
    all_gather x7, blocking collectives, local(): lax.all_gather(fresh_keys, 'blk', axis=0, tiled=True)  32.4 us
  transfers between devices with their start and end apart: 29, of which 23 were waited for; matrix products, arithmetic and copies ran while one was open for 5% of the time, Pallas kernels for 0%

profile of v1, /device:TPU:0, one launch (start us, length us, event | category | flops | bytes accessed | tf_op | source)
XLA Modules:
  0.0 606.6 jit_solution(3050480046043558497)
XLA Ops:
  6.5 4.2 constant_dynamic-slice_fusion.23
  10.8 6.1 %copy.202 = bf16[1,1536,3,384]{1,3,2,0:T(8,128)(2,1)} copy(bf16[1,1536,3,384]{3,1,2,0:T(8,128)(2,1)} %constant_dynamic-slice_fusion.23) | data formatting | bytes 7077888
  16.9 6.1 %copy.111 = bf16[1,1536,3,384]{1,3,2,0:T(8,128)(2,1)} copy(bf16[1,1536,3,384]{3,1,2,0:T(8,128)(2,1)} %param.39) | data formatting | bytes 7077888 | tf_op args[2]
  23.1 3.0 collective-permute-start.6
  30.2 5.6 all_gather.72
  37.6 36.0 %collective-permute-done.6 = bf16[1,384,1536]{2,1,0:T(8,128)(2,1)} collective-permute-done((bf16[1,384,1536]{2,1,0:T(8,128)(2,1)}, bf16[1,384,1536]{2,1,0:T(8,128)(2,1)}, u32[]{:S(2)}, u32[]{:S(2)}) %collective-permute-start.6) | collective-permute-done | bytes 1179680 | tf_op jit(solution)/shard_map/ppermute | solution.py:18
  75.8 52.6 %all-gather.9.cloned.1.call-done = bf16[1,3072,3,384]{1,3,2,0:T(8,128)(2,1)} async-done(((bf16[1,1536,3,384]{1,3,2,0:T(8,128)(2,1)}), bf16[1,3072,3,384]{1,3,2,0:T(8,128)(2,1)}) %all-gather.9.cloned.1.call-update) | async-done | bytes 7077904 | tf_op jit(solution)/shard_map/all_gather | solution.py:64
  128.4 92.3 %all-gather.7.cloned.1.call-done = bf16[1,3072,3,384]{1,3,2,0:T(8,128)(2,1)} async-done(((bf16[1,1536,3,384]{1,3,2,0:T(8,128)(2,1)}), bf16[1,3072,3,384]{1,3,2,0:T(8,128)(2,1)}) %all-gather.7.cloned.1.call-update) | async-done | bytes 7077904 | tf_op jit(solution)/shard_map/all_gather | solution.py:63
  220.7 5.2 conditional.14
  220.7 5.2 fusion.171
  226.3 4.5 all_gather.76
  230.8 5.0 all_gather.75
  239.0 19.7 %all-gather.11.cloned.1.call-done = bf16[1,384,3072]{2,1,0:T(8,128)(2,1)} async-done(((bf16[1,384,1536]{2,1,0:T(8,128)(2,1)}), bf16[1,384,3072]{2,1,0:T(8,128)(2,1)}) %all-gather.11.cloned.1.call-update) | async-done | bytes 2359312 | tf_op jit(solution)/shard_map/all_gather | solution.py:66
  263.7 18.3 %reduce-scatter.8.cloned.1.call-done = f32[8,3072]{1,0:T(8,128)} async-done(((f32[32,3072]{1,0:T(8,128)}), f32[8,3072]{1,0:T(8,128)}) %reduce-scatter.8.cloned.1.call-update) | async-done | bytes 98320 | tf_op jit(solution)/shard_map/reduce_scatter | solution.py:150
  282.9 3.4 collective-permute-start.7
  288.5 5.6 all_gather.78
  294.1 5.2 conditional.16
  294.1 5.2 fusion.174
  299.7 5.0 all_gather.80
  305.7 4.5 all_gather.79
  316.4 4.5 collective-permute-done.13
  320.9 13.4 %reduce-scatter.10.cloned.1.call-done = f32[8,3072]{1,0:T(8,128)} async-done(((f32[32,3072]{1,0:T(8,128)}), f32[8,3072]{1,0:T(8,128)}) %reduce-scatter.10.cloned.1.call-update) | async-done | bytes 98320 | tf_op jit(solution)/shard_map/reduce_scatter | solution.py:150
  335.3 3.4 collective-permute-start.8
  341.6 5.6 all_gather.81
  347.2 5.2 conditional.18
  347.2 5.2 fusion.178
  352.9 4.5 all_gather.83
  358.0 4.5 all_gather.82
  368.2 4.4 collective-permute-done.14
  372.6 14.4 %reduce-scatter.12.cloned.1.call-done = f32[8,3072]{1,0:T(8,128)} async-done(((f32[32,3072]{1,0:T(8,128)}), f32[8,3072]{1,0:T(8,128)}) %reduce-scatter.12.cloned.1.call-update) | async-done | bytes 98320 | tf_op jit(solution)/shard_map/reduce_scatter | solution.py:150
  387.9 3.4 collective-permute-start.9
  393.5 5.6 all_gather.84
  399.2 5.2 conditional.20
  399.2 5.2 fusion.182
  404.8 4.7 all_gather.86
  410.4 4.5 all_gather.85
  420.5 3.4 collective-permute-done.15
  423.9 15.2 %reduce-scatter.14.cloned.1.call-done = f32[8,3072]{1,0:T(8,128)} async-done(((f32[32,3072]{1,0:T(8,128)}), f32[8,3072]{1,0:T(8,128)}) %reduce-scatter.14.cloned.1.call-update) | async-done | bytes 98320 | tf_op jit(solution)/shard_map/reduce_scatter | solution.py:150
  440.0 3.4 collective-permute-start.10
  445.6 5.6 all_gather.87
  451.3 5.2 conditional.22
  451.3 5.2 fusion.186
  456.9 4.5 all_gather.89
  462.4 4.5 all_gather.88
  472.4 3.7 collective-permute-done.16
  476.1 15.6 %reduce-scatter.16.cloned.1.call-done = f32[8,3072]{1,0:T(8,128)} async-done(((f32[32,3072]{1,0:T(8,128)}), f32[8,3072]{1,0:T(8,128)}) %reduce-scatter.16.cloned.1.call-update) | async-done | bytes 98320 | tf_op jit(solution)/shard_map/reduce_scatter | solution.py:150
  492.6 3.4 collective-permute-start.11
  498.2 5.6 all_gather.90
  503.8 5.2 conditional.24
  503.8 5.2 fusion.190
  509.5 4.7 all_gather.92
  515.2 4.5 all_gather.91
  525.2 3.7 collective-permute-done.17
  528.9 14.8 %reduce-scatter.18.cloned.1.call-done = f32[8,3072]{1,0:T(8,128)} async-done(((f32[32,3072]{1,0:T(8,128)}), f32[8,3072]{1,0:T(8,128)}) %reduce-scatter.18.cloned.1.call-update) | async-done | bytes 98320 | tf_op jit(solution)/shard_map/reduce_scatter | solution.py:150
  544.6 3.4 collective-permute-start.12
  550.2 5.6 all_gather.93
  555.8 5.2 conditional.26
  555.8 5.2 fusion.194
  561.5 4.5 all_gather.95
  566.9 4.5 all_gather.94
  573.0 2.4 conditional.27
  573.0 2.3 fusion.196
  577.5 5.0 collective-permute-done.18
  582.5 15.5 %reduce-scatter.20.cloned.1.call-done = f32[8,3072]{1,0:T(8,128)} async-done(((f32[32,3072]{1,0:T(8,128)}), f32[8,3072]{1,0:T(8,128)}) %reduce-scatter.20.cloned.1.call-update) | async-done | bytes 98320 | tf_op jit(solution)/shard_map/reduce_scatter | solution.py:150
  (306 shorter events, 81.0 us)
Async XLA Ops:
  6.5 19.6 %copy-start = (bf16[2,384,1536]{2,1,0:T(8,128)(2,1)S(1)}, bf16[2,384,1536]{2,1,0:T(8,128)(2,1)}, u32[]{:S(2)}) copy-start(bf16[2,384,1536]{2,1,0:T(8,128)(2,1)} %param.42) | copy-start | bytes 7077892
  6.5 121.9 %all-gather.9.cloned.1.call-start = ((), (), s32[]{:S(2)}) async-start(), calls=%async_computation.15 | async-start | bytes 10616832 | tf_op jit(solution)/shard_map/all_gather | solution.py:64
  16.9 203.8 %all-gather.7.cloned.1.call-start = ((), (), s32[]{:S(2)}) async-start(), calls=%async_computation.14 | async-start | bytes 10616832 | tf_op jit(solution)/shard_map/all_gather | solution.py:63
  23.1 4.3 copy-start.11
  23.1 4.7 copy-start.12
  23.1 235.7 %all-gather.11.cloned.1.call-start = ((), (), s32[]{:S(2)}) async-start(), calls=%async_computation.16 | async-start | bytes 3538944 | tf_op jit(solution)/shard_map/all_gather | solution.py:66
  23.1 50.4 %collective-permute-start.6 = (bf16[1,384,1536]{2,1,0:T(8,128)(2,1)}, bf16[1,384,1536]{2,1,0:T(8,128)(2,1)}, u32[]{:S(2)}, u32[]{:S(2)}) collective-permute-start(bf16[1,384,1536]{2,1,0:T(8,128)(2,1)} %param.41), channel_id=1, source_target_pairs={{0,4},{4,0},{1,5},{5,1},{2,6},{6,2},{3,7},{7,3},{8,12},{12,8},{9,1... | collective-permute-start | bytes 3538952 | tf_op jit(solution)/shard_map/ppermute | solution.py:18
  27.2 2.0 copy-start.10
  27.2 9.2 %copy-start.14 = (f32[1,2,2,128]{3,2,1,0:T(2,128)S(1)}, f32[1,2,2,128]{3,2,1,0:T(2,128)}, u32[]{:S(2)}) copy-start(f32[1,2,2,128]{3,2,1,0:T(2,128)} %param.44) | copy-start | bytes 6148
  27.3 254.7 %reduce-scatter.8.cloned.1.call-start = ((), (), s32[]{:S(2)}) async-start(), calls=%async_computation.7 | async-start | bytes 491520 | tf_op jit(solution)/shard_map/reduce_scatter | solution.py:150
  75.8 445.4 %copy-start.2 = (bf16[2,48,8,1536]{3,2,0,1:T(8,128)(2,1)}, bf16[2,48,8,1536]{3,2,0,1:T(8,128)(2,1)S(1)}, u32[]{:S(2)}) copy-start(bf16[2,48,8,1536]{3,2,0,1:T(8,128)(2,1)S(1)} %copy.205) | copy-start | bytes 7077892
  260.9 0.8 copy-start.3
  261.7 72.7 %reduce-scatter.10.cloned.1.call-start = ((), (), s32[]{:S(2)}) async-start(), calls=%async_computation.8 | async-start | bytes 491520 | tf_op jit(solution)/shard_map/reduce_scatter | solution.py:150
  261.8 24.5 %collective-permute-start = (bf16[8,3072]{1,0:T(8,128)(2,1)S(1)}, bf16[8,3072]{1,0:T(8,128)(2,1)S(1)}, u32[]{:S(2)}, u32[]{:S(2)}) collective-permute-start(bf16[8,3072]{1,0:T(8,128)(2,1)S(1)} %bitcast.473), channel_id=1, source_target_pairs={{8,0},{16,8},{24,16},{9,1},{17,9},{25,17},{10,2},{18,10},{26,18},{... | collective-permute-start | bytes 147464 | tf_op jit(solution)/shard_map/ppermute | solution.py:32
  282.9 5.1 collective-permute-start.7
  299.2 12.0 %copy-start.20 = (f32[128]{0:T(128)S(1)}, f32[128]{0:T(128)}, u32[]{:S(2)}) copy-start(f32[128]{0:T(128)} %get-tuple-element.351) | copy-start | bytes 1540
  299.2 12.1 %copy-start.21 = (pred[256]{0:T(512)(128)(4,1)S(1)}, pred[256]{0:T(512)(128)(4,1)}, u32[]{:S(2)}) copy-start(pred[256]{0:T(512)(128)(4,1)} %compare_or_fusion) | copy-start | bytes 772
  312.4 0.7 copy-start.4
  313.2 73.8 %reduce-scatter.12.cloned.1.call-start = ((), (), s32[]{:S(2)}) async-start(), calls=%async_computation.9 | async-start | bytes 491520 | tf_op jit(solution)/shard_map/reduce_scatter | solution.py:150
  313.3 7.7 %collective-permute-start.13 = (bf16[8,3072]{1,0:T(8,128)(2,1)S(1)}, bf16[8,3072]{1,0:T(8,128)(2,1)S(1)}, u32[]{:S(2)}, u32[]{:S(2)}) collective-permute-start(bf16[8,3072]{1,0:T(8,128)(2,1)S(1)} %get-tuple-element.283), channel_id=1, source_target_pairs={{8,0},{16,8},{24,16},{9,1},{17,9},{25,17},{10,2},{18,10},{26,18},{... | collective-permute-start | bytes 147464 | tf_op jit(solution)/shard_map/ppermute | solution.py:32
  315.2 23.6 %collective-permute-start.1 = (bf16[8,3072]{1,0:T(8,128)(2,1)S(1)}, bf16[8,3072]{1,0:T(8,128)(2,1)S(1)}, u32[]{:S(2)}, u32[]{:S(2)}) collective-permute-start(bf16[8,3072]{1,0:T(8,128)(2,1)S(1)} %collective-permute-done), channel_id=1, source_target_pairs={{8,0},{16,8},{24,16},{9,1},{17,9},{25,17},{10,2},{18,10},{26,18},{... | collective-permute-start | bytes 147464 | tf_op jit(solution)/shard_map/ppermute | solution.py:32
  335.3 5.1 collective-permute-start.8
  352.4 10.7 %copy-start.18 = (f32[128]{0:T(128)S(1)}, f32[128]{0:T(128)}, u32[]{:S(2)}) copy-start(f32[128]{0:T(128)} %get-tuple-element.349) | copy-start | bytes 1540
  352.4 10.8 %copy-start.22 = (pred[256]{0:T(512)(128)(4,1)S(1)}, pred[256]{0:T(512)(128)(4,1)}, u32[]{:S(2)}) copy-start(pred[256]{0:T(512)(128)(4,1)} %compare_or_fusion) | copy-start | bytes 772
  363.8 2.7 copy-start.17
  363.8 29.7 %copy-start.13 = (f32[1,1,1,3072]{3,1,2,0:T(1,128)S(1)}, f32[1,1,1,3072]{3,1,2,0:T(1,128)}, u32[]{:S(2)}) copy-start(f32[1,1,1,3072]{3,1,2,0:T(1,128)} %get-tuple-element.328) | copy-start | bytes 36868
  364.3 0.7 copy-start.5
  365.1 74.0 %reduce-scatter.14.cloned.1.call-start = ((), (), s32[]{:S(2)}) async-start(), calls=%async_computation.10 | async-start | bytes 491520 | tf_op jit(solution)/shard_map/reduce_scatter | solution.py:150
  365.1 7.5 %collective-permute-start.14 = (bf16[8,3072]{1,0:T(8,128)(2,1)S(1)}, bf16[8,3072]{1,0:T(8,128)(2,1)S(1)}, u32[]{:S(2)}, u32[]{:S(2)}) collective-permute-start(bf16[8,3072]{1,0:T(8,128)(2,1)S(1)} %get-tuple-element.281), channel_id=1, source_target_pairs={{8,0},{16,8},{24,16},{9,1},{17,9},{25,17},{10,2},{18,10},{26,18},{... | collective-permute-start | bytes 147464 | tf_op jit(solution)/shard_map/ppermute | solution.py:32
  367.0 24.4 %collective-permute-start.2 = (bf16[8,3072]{1,0:T(8,128)(2,1)S(1)}, bf16[8,3072]{1,0:T(8,128)(2,1)S(1)}, u32[]{:S(2)}, u32[]{:S(2)}) collective-permute-start(bf16[8,3072]{1,0:T(8,128)(2,1)S(1)} %collective-permute-done.1), channel_id=1, source_target_pairs={{8,0},{16,8},{24,16},{9,1},{17,9},{25,17},{10,2},{18,10},{26,18},{... | collective-permute-start | bytes 147464 | tf_op jit(solution)/shard_map/ppermute | solution.py:32
  387.9 5.1 collective-permute-start.9
  404.3 11.6 %copy-start.19 = (f32[128]{0:T(128)S(1)}, f32[128]{0:T(128)}, u32[]{:S(2)}) copy-start(f32[128]{0:T(128)} %get-tuple-element.347) | copy-start | bytes 1540
  404.3 11.7 %copy-start.23 = (pred[256]{0:T(512)(128)(4,1)S(1)}, pred[256]{0:T(512)(128)(4,1)}, u32[]{:S(2)}) copy-start(pred[256]{0:T(512)(128)(4,1)} %compare_or_fusion) | copy-start | bytes 772
  416.6 2.7 copy-start.16
  417.1 0.7 copy-start.6
  417.9 73.8 %reduce-scatter.16.cloned.1.call-start = ((), (), s32[]{:S(2)}) async-start(), calls=%async_computation.11 | async-start | bytes 491520 | tf_op jit(solution)/shard_map/reduce_scatter | solution.py:150
  417.9 6.0 collective-permute-start.15
  419.2 24.2 %collective-permute-start.3 = (bf16[8,3072]{1,0:T(8,128)(2,1)S(1)}, bf16[8,3072]{1,0:T(8,128)(2,1)S(1)}, u32[]{:S(2)}, u32[]{:S(2)}) collective-permute-start(bf16[8,3072]{1,0:T(8,128)(2,1)S(1)} %collective-permute-done.2), channel_id=1, source_target_pairs={{8,0},{16,8},{24,16},{9,1},{17,9},{25,17},{10,2},{18,10},{26,18},{... | collective-permute-start | bytes 147464 | tf_op jit(solution)/shard_map/ppermute | solution.py:32
  440.0 5.1 collective-permute-start.10
  468.5 2.7 copy-start.15
  469.0 0.7 copy-start.7
  469.8 73.9 %reduce-scatter.18.cloned.1.call-start = ((), (), s32[]{:S(2)}) async-start(), calls=%async_computation.12 | async-start | bytes 491520 | tf_op jit(solution)/shard_map/reduce_scatter | solution.py:150
  469.8 6.3 %collective-permute-start.16 = (bf16[8,3072]{1,0:T(8,128)(2,1)S(1)}, bf16[8,3072]{1,0:T(8,128)(2,1)S(1)}, u32[]{:S(2)}, u32[]{:S(2)}) collective-permute-start(bf16[8,3072]{1,0:T(8,128)(2,1)S(1)} %get-tuple-element.277), channel_id=1, source_target_pairs={{8,0},{16,8},{24,16},{9,1},{17,9},{25,17},{10,2},{18,10},{26,18},{... | collective-permute-start | bytes 147464 | tf_op jit(solution)/shard_map/ppermute | solution.py:32
  471.1 24.9 %collective-permute-start.4 = (bf16[8,3072]{1,0:T(8,128)(2,1)S(1)}, bf16[8,3072]{1,0:T(8,128)(2,1)S(1)}, u32[]{:S(2)}, u32[]{:S(2)}) collective-permute-start(bf16[8,3072]{1,0:T(8,128)(2,1)S(1)} %collective-permute-done.3), channel_id=1, source_target_pairs={{8,0},{16,8},{24,16},{9,1},{17,9},{25,17},{10,2},{18,10},{26,18},{... | collective-permute-start | bytes 147464 | tf_op jit(solution)/shard_map/ppermute | solution.py:32
  492.6 5.1 collective-permute-start.11
  521.8 0.7 copy-start.8
  522.6 75.4 %reduce-scatter.20.cloned.1.call-start = ((), (), s32[]{:S(2)}) async-start(), calls=%async_computation.13 | async-start | bytes 491520 | tf_op jit(solution)/shard_map/reduce_scatter | solution.py:150
  522.6 6.3 %collective-permute-start.17 = (bf16[8,3072]{1,0:T(8,128)(2,1)S(1)}, bf16[8,3072]{1,0:T(8,128)(2,1)S(1)}, u32[]{:S(2)}, u32[]{:S(2)}) collective-permute-start(bf16[8,3072]{1,0:T(8,128)(2,1)S(1)} %get-tuple-element.275), channel_id=1, source_target_pairs={{8,0},{16,8},{24,16},{9,1},{17,9},{25,17},{10,2},{18,10},{26,18},{... | collective-permute-start | bytes 147464 | tf_op jit(solution)/shard_map/ppermute | solution.py:32
  523.9 24.1 %collective-permute-start.5 = (bf16[8,3072]{1,0:T(8,128)(2,1)S(1)}, bf16[8,3072]{1,0:T(8,128)(2,1)S(1)}, u32[]{:S(2)}, u32[]{:S(2)}) collective-permute-start(bf16[8,3072]{1,0:T(8,128)(2,1)S(1)} %collective-permute-done.4), channel_id=1, source_target_pairs={{8,0},{16,8},{24,16},{9,1},{17,9},{25,17},{10,2},{18,10},{26,18},{... | collective-permute-start | bytes 147464 | tf_op jit(solution)/shard_map/ppermute | solution.py:32
  544.6 5.1 collective-permute-start.12
  573.0 26.5 %copy-start.1 = (bf16[2,384,1536]{2,1,0:T(8,128)(2,1)S(1)}, bf16[2,384,1536]{2,1,0:T(8,128)(2,1)}, u32[]{:S(2)}) copy-start(bf16[2,384,1536]{2,1,0:T(8,128)(2,1)} %param.42) | copy-start | bytes 7077892
  575.4 0.8 copy-start.9
  576.1 6.3 %collective-permute-start.18 = (bf16[8,3072]{1,0:T(8,128)(2,1)S(1)}, bf16[8,3072]{1,0:T(8,128)(2,1)S(1)}, u32[]{:S(2)}, u32[]{:S(2)}) collective-permute-start(bf16[8,3072]{1,0:T(8,128)(2,1)S(1)} %get-tuple-element.273), channel_id=1, source_target_pairs={{8,0},{16,8},{24,16},{9,1},{17,9},{25,17},{10,2},{18,10},{26,18},{... | collective-permute-start | bytes 147464 | tf_op jit(solution)/shard_map/ppermute | solution.py:32
Sparse Core Ops, SparseCore 0:
  17.0 111.3 all-gather.8
  129.9 90.7 all-gather.6
  222.3 36.4 all-gather.10
  261.8 20.0 reduce-scatter.7
  313.3 20.9 reduce-scatter.9
  365.2 21.7 reduce-scatter.11
  418.0 21.0 reduce-scatter.13
  469.9 21.7 reduce-scatter.15
  522.7 20.9 reduce-scatter.17
  576.3 21.6 reduce-scatter.19
